TPU v7x, 128 devices: a whole 4x4x4 slice. The times are simulated.
128 devices in a mesh: batch: 16 (over x, z), proto: 8 (over y, core).
Axes of the slice: x: 4, y: 4, z: 4, core: 2. Of those that a mesh axis runs over, the one named last changes fastest.
Arguments:
- student_feats: bfloat16 [8192, 256], P('batch'), may hold values from -4 to 9
- teacher_feats: bfloat16 [8192, 256], P('batch'), may hold values from -3 to 3
- protos: bfloat16 [256, 65536], P(None, 'proto'), may hold values from -1 to 4
- teacher_protos: bfloat16 [256, 65536], P(None, 'proto'), may hold values from -3 to 3
Outputs:
- grad_feats: float32 [8192, 256], P('batch')
- grad_protos: float32 [256, 65536], P('batch', 'proto')
All inputs are finite; a program needn't handle non-finite values.
Results may differ from a plain program's by a relative error of at most 0.0064.
Values sent between devices are 32-bit elements; how exact they have to be, the bound alone decides.
No kernel may reach another device: no remote copies, remote signals or barrier semaphores. Data moves between devices by JAX's collectives and lax.ppermute only.
A program may use at most 128 MiB of HBM per device.

v0:
```python
import jax
import jax.numpy as jnp
from jax import lax
from jax.sharding import PartitionSpec as P

ITERS = 3


EPSILON = 1e-06
TEACHER_TEMP = 0.04
STUDENT_TEMP = 0.1


def unit_rows(values):
    wide = values.astype(jnp.float32)
    norms = jnp.sqrt(jnp.sum(wide * wide, axis=1, keepdims=True) + EPSILON)
    return ((wide / norms).astype(jnp.bfloat16), norms)


def unit_columns(values):
    wide = values.astype(jnp.float32)
    norms = jnp.sqrt(jnp.sum(wide * wide, axis=0, keepdims=True) + EPSILON)
    return ((wide / norms).astype(jnp.bfloat16), norms)


def on_device(student_feats, teacher_feats, protos, teacher_protos):
    rows_here = student_feats.shape[0]
    width = protos.shape[0]
    total_rows = rows_here * lax.axis_size("batch")
    total_protos = protos.shape[1] * lax.axis_size("proto")
    teach_z, unused_one = unit_rows(teacher_feats)
    teach_w, unused_two = unit_columns(teacher_protos)
    student_z, student_norm = unit_rows(student_feats)
    student_w, proto_norm = unit_columns(protos)
    energy = jnp.exp(jnp.dot(teach_z, teach_w, preferred_element_type=jnp.float32) / TEACHER_TEMP)
    assign = energy
    for step_index in range(ITERS):
        col_part = jnp.sum(assign, axis=0)
        col_total = lax.psum(col_part, "batch")
        assign = assign / (total_protos * col_total)[None, :]
        row_part = jnp.sum(assign, axis=1)
        row_total = lax.psum(row_part, "proto")
        assign = assign / (total_rows * row_total)[:, None]
    targets = assign * total_rows
    raw = jnp.dot(student_z, student_w, preferred_element_type=jnp.float32)
    expo = jnp.exp(raw / STUDENT_TEMP)
    totals = lax.psum(jnp.sum(expo, axis=1), "proto")
    prob = expo / totals[:, None]
    dscore = ((prob - targets) / STUDENT_TEMP).astype(jnp.bfloat16)
    feat_part = lax.dot_general(
        dscore, student_w, (((1,), (1,)), ((), ())), preferred_element_type=jnp.float32
    )
    feat_sum = lax.psum(feat_part, "proto")
    zs_wide = student_z.astype(jnp.float32)
    along = jnp.sum(zs_wide * feat_sum, axis=1, keepdims=True)
    grad_feats = (feat_sum - zs_wide * along) / student_norm
    share = width // lax.axis_size("batch")
    offset = lax.axis_index("batch") * share
    w_mine = lax.dynamic_slice_in_dim(student_w, offset, share, 0).astype(jnp.float32)
    mine = lax.psum_scatter(
        lax.dot_general(
            student_z, dscore, (((0,), (0,)), ((), ())), preferred_element_type=jnp.float32
        ),
        "batch",
        scatter_dimension=0,
        tiled=True,
    )
    dots = lax.psum(jnp.sum(w_mine * mine, axis=0), "batch")
    grad_protos = (mine - w_mine * dots[None, :]) / proto_norm
    return (grad_feats, grad_protos)


def solution(mesh):
    return jax.shard_map(
        on_device,
        mesh=mesh,
        in_specs=(P("batch", None), P("batch", None), P(None, "proto"), P(None, "proto")),
        out_specs=(P("batch", None), P("batch", "proto")),
        check_vma=False,
    )
```

profile of v0, /device:TPU:0, one launch (start us, length us, event | category | flops | bytes accessed | tf_op | source)
XLA Modules:
  0.0 519.7 jit_solution(3526527709298161399)
XLA Ops:
  8.0 0.0 all-reduce.3.cloned.1.call-start
  8.0 3.1 fusion.16
  11.1 1.1 fusion.22
  12.2 11.5 %fusion.36 = (f32[8192]{0:T(1024)S(1)}, f32[512,8192]{1,0:T(8,128)}) fusion(bf16[256,8192]{1,0:T(8,128)(2,1)} %param.7, f32[8192]{0:T(1024)S(1)} %add_sqrt_fusion, bf16[512,256]{1,0:T(8,128)(2,1)} %param.5, f32[512]{0:T(512)S(1)} %add_sqrt_fusion.2), kind=kOutput, calls=%fused_computation.60 | convolution fusion | flops 2162548736 | bytes 21301248 | tf_op jit(solution)/shard_map/dot_general | solution.py:35
  23.8 75.7 %psum.64 = f32[8192]{0:T(1024)S(1)} all-reduce(f32[8192]{0:T(1024)S(1)} %get-tuple-element.4), channel_id=1, replica_groups=mesh['batch'=16,'proto'=8] {'batch'}, use_global_device_ids=true, to_apply=%region_7.0 | all-reduce | flops 8192 | bytes 65536 | tf_op jit(solution)/shard_map/psum | solution.py:39
  99.5 7.0 %divide_reduce_fusion = f32[512]{0:T(512)S(1)} fusion(f32[512,8192]{1,0:T(8,128)} %get-tuple-element.5, f32[8192]{0:T(1024)S(1)} %broadcast_multiply_fusion.2), kind=kLoop, calls=%fused_computation.14 | loop fusion | flops 8388096 | bytes 16812032 | tf_op jit(solution)/shard_map/reduce_sum | solution.py:41
  106.5 12.4 %psum.65 = f32[512]{0:T(512)S(1)} all-reduce(f32[512]{0:T(512)S(1)} %divide_reduce_fusion), channel_id=1, replica_groups=mesh['batch'=16,'proto'=8] {'proto'}, use_global_device_ids=true, to_apply=%region_9.0 | all-reduce | flops 512 | bytes 4096 | tf_op jit(solution)/shard_map/psum | solution.py:42
  118.9 8.4 %fusion.9 = f32[8192]{0:T(1024)S(1)} fusion(f32[512,8192]{1,0:T(8,128)} %get-tuple-element.5, f32[512]{0:T(512)S(1)} %broadcast_multiply_fusion.5, f32[8192]{0:T(1024)S(1)} %broadcast_multiply_fusion.2), kind=kLoop, calls=%fused_computation.15 | loop fusion | flops 12574720 | bytes 16844800 | tf_op jit(solution)/shard_map/reduce_sum | solution.py:38
  127.4 69.7 %psum.66 = f32[8192]{0:T(1024)S(1)} all-reduce(f32[8192]{0:T(1024)S(1)} %fusion.9), channel_id=1, replica_groups=mesh['batch'=16,'proto'=8] {'batch'}, use_global_device_ids=true, to_apply=%region_11.0 | all-reduce | flops 8192 | bytes 65536 | tf_op jit(solution)/shard_map/psum | solution.py:39
  197.1 8.7 %fusion.10 = f32[512]{0:T(512)S(1)} fusion(f32[512,8192]{1,0:T(8,128)} %get-tuple-element.5, f32[8192]{0:T(1024)S(1)} %broadcast_multiply_fusion.1, f32[512]{0:T(512)S(1)} %broadcast_multiply_fusion.5, f32[8192]{0:T(1024)S(1)} %broadcast_multiply_fusion.2), kind=kLoop, calls=%fused_computation.16 | loop fusion | flops 16776704 | bytes 16846848 | tf_op jit(solution)/shard_map/reduce_sum | solution.py:41
  205.8 12.4 %psum.67 = f32[512]{0:T(512)S(1)} all-reduce(f32[512]{0:T(512)S(1)} %fusion.10), channel_id=1, replica_groups=mesh['batch'=16,'proto'=8] {'proto'}, use_global_device_ids=true, to_apply=%region_13.0 | all-reduce | flops 512 | bytes 4096 | tf_op jit(solution)/shard_map/psum | solution.py:42
  218.2 7.8 %fusion.11 = f32[8192]{0:T(1024)S(1)} fusion(f32[512,8192]{1,0:T(8,128)} %get-tuple-element.5, f32[512]{0:T(512)S(1)} %broadcast_multiply_fusion.4, f32[8192]{0:T(1024)S(1)} %broadcast_multiply_fusion.1, f32[512]{0:T(512)S(1)} %broadcast_multiply_fusion.5, f32[8192]{0:T(1024)S(1)} %broadcast_multiply_fusion.2), kind=kLoop, calls=%fused_computation.17 | loop fusion | flops 20963328 | bytes 16879616 | tf_op jit(solution)/shard_map/reduce_sum | solution.py:38
  226.0 0.0 copy-start.4
  226.0 69.7 %psum.68 = f32[8192]{0:T(1024)S(1)} all-reduce(f32[8192]{0:T(1024)S(1)} %fusion.11), channel_id=1, replica_groups=mesh['batch'=16,'proto'=8] {'batch'}, use_global_device_ids=true, to_apply=%region_15.0 | all-reduce | flops 8192 | bytes 65536 | tf_op jit(solution)/shard_map/psum | solution.py:39
  295.7 0.0 copy-start.3
  295.7 8.5 %fusion.12 = f32[512]{0:T(512)S(1)} fusion(f32[512,8192]{1,0:T(8,128)} %get-tuple-element.5, f32[8192]{0:T(1024)S(1)} %broadcast_multiply_fusion, f32[512]{0:T(512)S(1)} %broadcast_multiply_fusion.4, f32[8192]{0:T(1024)S(1)} %broadcast_multiply_fusion.1, f32[512]{0:T(512)S(1)} %broadcast_multiply_fusion.5, f32[8192]{0:T(1024)S(1)} %broadcast_multiply_fusion.2), kind=kLoop, calls=%fused_computation.18 | loop fusion | flops 25165312 | bytes 16881664 | tf_op jit(solution)/shard_map/reduce_sum | solution.py:41
  304.2 0.0 copy-done.3
  304.2 0.9 fusion.14
  305.1 1.0 fusion.15
  306.1 0.0 copy-done.4
  306.1 0.0 copy-start.1
  306.1 0.1 fusion.20
  306.3 1.9 copy-done.1
  308.2 7.4 %fusion.13 = (f32[512]{0:T(512)S(1)}, f32[512,8192]{1,0:T(8,128)}) fusion(bf16[256,8192]{1,0:T(8,128)(2,1)S(1)} %fusion.15, bf16[512,256]{1,0:T(8,128)(2,1)S(1)} %copy-done.4, f32[512]{0:T(512)S(1)} %add_sqrt_fusion.3), kind=kOutput, calls=%fused_computation.19 | convolution fusion | flops 2156264960 | bytes 21237760 | tf_op jit(solution)/shard_map/dot_general | solution.py:45
  315.6 12.6 %all-reduce = (f32[512]{0:T(512)S(1)}, f32[512]{0:T(512)S(1)}) all-reduce(f32[512]{0:T(512)S(1)} %fusion.12, f32[512]{0:T(512)S(1)} %get-tuple-element.6), channel_id=1, replica_groups=mesh['batch'=16,'proto'=8] {'proto'}, use_global_device_ids=true, to_apply=%region_17.0 | all-reduce | flops 1024 | bytes 8192 | tf_op jit(solution)/shard_map/psum | solution.py:42
  328.2 0.0 copy-start.2
  328.2 14.4 %multiply_convert_fusion = bf16[512,8192]{1,0:T(8,128)(2,1)S(1)} fusion(f32[512,8192]{1,0:T(8,128)} %get-tuple-element.5, f32[512,8192]{1,0:T(8,128)} %get-tuple-element.7, f32[512]{0:T(512)S(1)} %broadcast_multiply_fusion.3, f32[8192]{0:T(1024)S(1)} %broadcast_multiply_fusion, f32[512]{0:T(512)S(1)} %broadcast_multiply_fusion.4, ...), kind=kLoop, calls=%fused_computation.11 | loop fusion | flops 50331648 | bytes 42049536 | tf_op jit(solution)/shard_map/convert_element_type | solution.py:49
  342.6 0.0 copy-start
  342.6 3.2 copy-done
  345.8 0.0 copy-done.2
  345.8 3.2 fusion.37
  348.9 0.0 all-reduce.3.cloned.1.call-update
  349.0 0.0 reduce-scatter.2.cloned.1.call-start
  349.0 9.1 %fusion.32 = f32[256,8192]{1,0:T(8,128)} fusion(bf16[512,8192]{1,0:T(8,128)(2,1)} %copy-done, bf16[512,256]{1,0:T(8,128)(2,1)S(1)} %copy-done.4, f32[512]{0:T(512)S(1)} %add_sqrt_fusion.3), kind=kOutput, calls=%fused_computation.58 | convolution fusion | flops 2147876864 | bytes 17041408 | tf_op jit(solution)/shard_map/dot_general | solution.py:61
  358.2 0.0 reduce-scatter.2.cloned.1.call-update
  358.2 45.9 %all-reduce.3.cloned.1.call-done = f32[512,256]{1,0:T(8,128)} async-done(((f32[512,256]{1,0:T(8,128)}), f32[512,256]{1,0:T(8,128)}) %all-reduce.3.cloned.1.call-update) | async-done | bytes 524304 | tf_op jit(solution)/shard_map/psum | solution.py:53
  404.1 1.3 fusion.24
  405.3 2.1 fusion.26
  407.4 29.5 %reduce-scatter.2.cloned.1.call-done = f32[16,8192]{1,0:T(8,128)} async-done(((f32[256,8192]{1,0:T(8,128)}), f32[16,8192]{1,0:T(8,128)}) %reduce-scatter.2.cloned.1.call-update) | async-done | bytes 524304 | tf_op jit(solution)/shard_map/reduce_scatter | solution.py:60
  436.9 1.2 fusion.27
  438.1 72.1 %psum.71 = f32[8192]{0:T(1024)S(1)} all-reduce(f32[8192]{0:T(1024)S(1)} %fusion.27), channel_id=1, replica_groups=mesh['batch'=16,'proto'=8] {'batch'}, use_global_device_ids=true, to_apply=%region_22.0 | all-reduce | flops 8192 | bytes 65536 | tf_op jit(solution)/shard_map/psum | solution.py:68
  510.2 2.0 fusion.29
  (10 shorter events, 0.1 us)
Async XLA Ops:
  8.0 396.1 %all-reduce.3.cloned.1.call-start = ((), (), s32[]{:S(2)}) async-start(), calls=%async_computation.1 | async-start | bytes 1048576 | tf_op jit(solution)/shard_map/psum | solution.py:53
  226.0 80.1 %copy-start.4 = (bf16[512,256]{1,0:T(8,128)(2,1)S(1)}, bf16[512,256]{1,0:T(8,128)(2,1)}, u32[]{:S(2)}) copy-start(bf16[512,256]{1,0:T(8,128)(2,1)} %param.4) | copy-start | bytes 786436
  295.7 8.5 %copy-start.3 = (bf16[256,8192]{1,0:T(8,128)(2,1)S(1)}, bf16[256,8192]{1,0:T(8,128)(2,1)}, u32[]{:S(2)}) copy-start(bf16[256,8192]{1,0:T(8,128)(2,1)} %param.6) | copy-start | bytes 12582916
  306.1 2.0 copy-start.1
  328.2 17.6 %copy-start.2 = (bf16[256,8192]{1,0:T(8,128)(2,1)S(1)}, bf16[256,8192]{1,0:T(8,128)(2,1)}, u32[]{:S(2)}) copy-start(bf16[256,8192]{1,0:T(8,128)(2,1)} %copy-done.1) | copy-start | bytes 12582916
  342.6 3.2 copy-start
  349.0 88.0 %reduce-scatter.2.cloned.1.call-start = ((), (), s32[]{:S(2)}) async-start(), calls=%async_computation.2 | async-start | bytes 8912896 | tf_op jit(solution)/shard_map/reduce_scatter | solution.py:60
Sparse Core Ops, SparseCore 0:
  349.1 54.9 all-reduce.2
Sparse Core Ops, SparseCore 1:
  358.3 78.6 reduce-scatter.1
where the time goes:
time: 520 us
  blocking collectives  325 us (62%)
  waiting for transfers between devices  75.4 us (15%)
  other arithmetic  67.6 us (13%)
  matrix products  31.2 us (6%)
  between operations  15.6 us (3%)
    psum x3, blocking collectives, on_device(): col_total = lax.psum(col_part, 'batch')  215 us
    psum x1, blocking collectives, on_device(): dots = lax.psum(jnp.sum(w_mine * mine, axis=0), 'batch')  72.1 us
    psum x1, waiting for transfers between devices, on_device(): feat_sum = lax.psum(feat_part, 'proto')  45.9 us
    psum x3, blocking collectives, on_device(): row_total = lax.psum(row_part, 'proto')  37.5 us
    reduce_scatter x1, waiting for transfers between devices, on_device(): lax.psum_scatter(lax.dot_general(student_z, dscore, (((0,), (0,)), ((), (...  29.5 us
    reduce_sum x3, other arithmetic, on_device(): row_part = jnp.sum(assign, axis=1)  24.2 us
    reduce_sum x2, other arithmetic, on_device(): col_part = jnp.sum(assign, axis=0)  16.2 us
    convert_element_type x1, other arithmetic, on_device(): dscore = ((prob - targets) / STUDENT_TEMP).astype(jnp.bfloat16)  14.4 us
  transfers between devices with their start and end apart: 2, of which 2 were waited for; matrix products, arithmetic and copies ran while one was open for 2% of the time, Pallas kernels for 0%

commit v1 on v0

v1 whole, which is shorter than its diff:
```python
import functools

import jax
import jax.numpy as jnp
from jax import lax
from jax.experimental import pallas as pl
from jax.experimental.pallas import tpu as pltpu
from jax.sharding import Mesh
from jax.sharding import PartitionSpec as P

EPSILON = 1e-06
TEACHER_SCALE = 25.0
STUDENT_SCALE = 10.0
LOG2E = 1.4426950408889634
SIZES = {"x": 4, "z": 4, "y": 4, "core": 2}
BATCH = ("x", "z")
PROTO = ("y", "core")
WHOLE = pl.BlockSpec(memory_space=pltpu.VMEM)
F32 = jnp.float32
BF16 = jnp.bfloat16


def params(mib):
    return pltpu.CompilerParams(vmem_limit_bytes=mib << 20)


def in_vmem(value):
    return pltpu.with_memory_space_constraint(value, pltpu.VMEM)


def unit_rows(values):
    wide = values.astype(F32)
    norms = jnp.sqrt(jnp.sum(wide * wide, axis=1, keepdims=True) + EPSILON)
    return (wide / norms).astype(BF16), norms


def unit_columns(values):
    wide = values.astype(F32)
    norms = jnp.sqrt(jnp.sum(wide * wide, axis=0, keepdims=True) + EPSILON)
    return (wide * (1.0 / norms)).astype(BF16), norms


def columns_of(step, size):
    return pl.ds(pl.multiple_of(step * size, size), size)


def across(row, lanes=128):
    return jnp.broadcast_to(row, (lanes, row.shape[1])).T


def two_terms(row):
    high = row.astype(BF16).astype(F32)
    place = lax.broadcasted_iota(jnp.int32, (16, row.shape[1]), 0)
    return jnp.where(place == 0, high, jnp.where(place == 1, row - high, 0.0)).astype(BF16)


def energy_kernel(feats, protos, energy, col_sum, *, size):
    here = columns_of(pl.program_id(0), size)
    unit, _ = unit_columns(protos[...])
    score = jnp.dot(feats[...], unit, preferred_element_type=F32)
    value = jnp.exp2(score * (TEACHER_SCALE * LOG2E))
    energy[:, here] = value.astype(BF16)
    col_sum[:, here] = jnp.sum(value, axis=0, keepdims=True)


def energy_call(feats, protos, size=1024):
    rows, width = feats.shape
    count = protos.shape[1]
    return pl.pallas_call(
        functools.partial(energy_kernel, size=size),
        grid=(count // size,),
        in_specs=[pl.BlockSpec((rows, width), lambda i: (0, 0)), pl.BlockSpec((width, size), lambda i: (0, i))],
        out_specs=[WHOLE, WHOLE],
        out_shape=[pltpu.VMEM((rows, count), BF16), jax.ShapeDtypeStruct((1, count), F32)],
        compiler_params=params(12),
        name="energy",
    )(feats, protos)


def student_kernel(feats, protos, expo, unit_out, norm_out, row_sum, total, *, size):
    step = pl.program_id(0)
    here = columns_of(step, size)
    unit, norm = unit_columns(protos[...])
    unit_out[:, here] = unit
    norm_out[:, here] = norm
    score = jnp.dot(feats[...], unit, preferred_element_type=F32)
    value = jnp.exp2(score * (STUDENT_SCALE * LOG2E))
    expo[:, here] = value.astype(BF16)
    lanes = value[:, :128]
    for tile in range(1, size // 128):
        lanes = lanes + value[:, tile * 128 : (tile + 1) * 128]

    @pl.when(step == 0)
    def _():
        total[...] = lanes

    @pl.when(step > 0)
    def _():
        total[...] += lanes

    @pl.when(step == pl.num_programs(0) - 1)
    def _():
        row_sum[...] = jnp.sum(total[...].T, axis=0, keepdims=True)


def student_call(feats, protos, size=1024):
    rows, width = feats.shape
    count = protos.shape[1]
    return pl.pallas_call(
        functools.partial(student_kernel, size=size),
        grid=(count // size,),
        in_specs=[pl.BlockSpec((rows, width), lambda i: (0, 0)), pl.BlockSpec((width, size), lambda i: (0, i))],
        out_specs=[WHOLE] * 4,
        out_shape=[
            pltpu.VMEM((rows, count), BF16),
            pltpu.VMEM((width, count), BF16),
            jax.ShapeDtypeStruct((1, count), F32),
            jax.ShapeDtypeStruct((1, rows), F32),
        ],
        scratch_shapes=[pltpu.VMEM((rows, 128), F32)],
        compiler_params=params(12),
        name="student",
    )(feats, protos)


def row_kernel(energy, col_total, row_part, *, total_protos, size=1024):
    rows, count = energy.shape
    total = jnp.zeros((16, rows), F32)
    for at in range(0, count, size):
        scale = two_terms(1.0 / (total_protos * col_total[:, at : at + size]))
        total = total + lax.dot_general(
            scale, energy[:, at : at + size], (((1,), (1,)), ((), ())), preferred_element_type=F32
        )
    row_part[...] = jnp.sum(total, axis=0, keepdims=True)


def row_call(energy, col_total, total_protos):
    return pl.pallas_call(
        functools.partial(row_kernel, total_protos=total_protos),
        in_specs=[WHOLE, WHOLE],
        out_specs=WHOLE,
        out_shape=jax.ShapeDtypeStruct((1, energy.shape[0]), F32),
        compiler_params=params(4),
        name="row_pass",
    )(in_vmem(energy), col_total)


def col_kernel(energy, row_total, col_part, *, total_rows, size=1024):
    scale = two_terms(1.0 / (total_rows * row_total[...]))
    for at in range(0, energy.shape[1], size):
        part = jnp.dot(scale, energy[:, at : at + size], preferred_element_type=F32)
        col_part[:, at : at + size] = jnp.sum(part, axis=0, keepdims=True)


def col_call(energy, row_total, total_rows):
    return pl.pallas_call(
        functools.partial(col_kernel, total_rows=total_rows),
        in_specs=[WHOLE, WHOLE],
        out_specs=WHOLE,
        out_shape=jax.ShapeDtypeStruct((1, energy.shape[1]), F32),
        compiler_params=params(4),
        name="col_pass",
    )(in_vmem(energy), row_total)


def grad_kernel(
    energy, expo, feats, unit, norm, col_total, row_total, soft_total, feat_part, grad, row_scale, soft_scale,
    *, total_protos, size,
):
    step = pl.program_id(0)
    here = columns_of(step, size)

    @pl.when(step == 0)
    def _():
        row_scale[...] = across(STUDENT_SCALE / row_total[...])
        soft_scale[...] = across(STUDENT_SCALE / soft_total[...])

    col_scale = 1.0 / (total_protos * col_total[:, here])
    target = energy[:, here].astype(F32) * col_scale
    prob = expo[:, here].astype(F32)
    wide = size // 128
    rows_r = jnp.concatenate([row_scale[...]] * wide, axis=1)
    rows_s = jnp.concatenate([soft_scale[...]] * wide, axis=1)
    dscore = (prob * rows_s - target * rows_r).astype(BF16)
    weights = unit[:, here]
    part = lax.dot_general(dscore, weights, (((1,), (1,)), ((), ())), preferred_element_type=F32)

    @pl.when(step == 0)
    def _():
        feat_part[...] = part

    @pl.when(step > 0)
    def _():
        feat_part[...] += part

    proto_part = lax.dot_general(feats[...], dscore, (((0,), (0,)), ((), ())), preferred_element_type=F32)
    wide_unit = weights.astype(F32)
    dots = jnp.sum(wide_unit * proto_part, axis=0, keepdims=True)
    grad[...] = (proto_part - wide_unit * dots) * (1.0 / norm[:, here])


def grad_call(energy, expo, feats, unit, norm, col_total, row_total, soft_total, total_protos, size=1024):
    rows, count = energy.shape
    width = unit.shape[0]
    return pl.pallas_call(
        functools.partial(grad_kernel, total_protos=total_protos, size=size),
        grid=(count // size,),
        in_specs=[WHOLE] * 8,
        out_specs=[WHOLE, pl.BlockSpec((width, size), lambda i: (0, i))],
        out_shape=[jax.ShapeDtypeStruct((rows, width), F32), jax.ShapeDtypeStruct((width, count), F32)],
        scratch_shapes=[pltpu.VMEM((rows, 128), F32)] * 2,
        compiler_params=params(16),
        name="grad",
    )(in_vmem(energy), in_vmem(expo), feats, in_vmem(unit), norm, col_total, row_total, soft_total)


def shifted(value, axis, shift):
    size = SIZES[axis]
    return lax.ppermute(value, axis, [(i, (i + shift) % size) for i in range(size)])


def ring_sum(value, axis):
    parts = [shifted(value, axis, shift) for shift in ((1, 3, 2) if SIZES[axis] == 4 else (1,))]
    for part in parts:
        value = value + part
    return value


def summed(value, axes):
    for axis in axes:
        value = ring_sum(value, axis)
    return value


def on_device(student_feats, teacher_feats, protos, teacher_protos):
    rows = student_feats.shape[0]
    total_rows = rows * 16
    total_protos = protos.shape[1] * 8
    teacher_unit, _ = unit_rows(teacher_feats)
    student_unit, student_norm = unit_rows(student_feats)
    energy, col_part = energy_call(teacher_unit, teacher_protos)
    col_total = summed(col_part, BATCH)
    expo, unit, norm, soft_part = student_call(student_unit, protos)
    row_part = row_call(energy, col_total, total_protos)
    both = summed(jnp.concatenate([row_part, soft_part], axis=0), ("core", "y"))
    row_total, soft_total = both[:1], both[1:]
    for _ in range(2):
        col_total = summed(col_call(energy, row_total, total_rows), BATCH)
        row_total = summed(row_call(energy, col_total, total_protos), ("core", "y"))
    feat_part, grad_part = grad_call(
        energy, expo, student_unit, unit, norm, col_total, row_total, soft_total, total_protos
    )
    grad_protos = lax.psum_scatter(grad_part, BATCH, scatter_dimension=0, tiled=True)

    core = lax.axis_index("core")
    half = rows // 2
    mine = lax.dynamic_slice_in_dim(feat_part, core * half, half, 0)
    other = lax.dynamic_slice_in_dim(feat_part, (1 - core) * half, half, 0)
    feat_sum = ring_sum(mine + shifted(other, "core", 1), "y")
    unit_here = lax.dynamic_slice_in_dim(student_unit, core * half, half, 0).astype(F32)
    norm_here = lax.dynamic_slice_in_dim(student_norm, core * half, half, 0)
    along = jnp.sum(unit_here * feat_sum, axis=1, keepdims=True)
    grad_here = (feat_sum - unit_here * along) / norm_here
    grad_there = shifted(grad_here, "core", 1)
    first = jnp.where(core == 0, grad_here, grad_there)
    second = jnp.where(core == 0, grad_there, grad_here)
    return jnp.concatenate([first, second], axis=0), grad_protos


def solution(mesh):
    split = Mesh(mesh.devices.reshape(4, 4, 4, 2), ("x", "z", "y", "core"))
    return jax.shard_map(
        on_device,
        mesh=split,
        in_specs=(P(BATCH, None), P(BATCH, None), P(None, PROTO), P(None, PROTO)),
        out_specs=(P(BATCH, None), P(BATCH, PROTO)),
        check_vma=False,
    )
```

time: 520 us -> 216 us (0.42)
  blocking collectives: 325 us -> 0 us
  other arithmetic: 67.6 us -> 5.99 us
  starting transfers between devices: 0.08 us -> 42.1 us
  waiting for transfers between devices: 75.4 us -> 113 us
  Pallas kernels: 0 us -> 33.2 us
  matrix products: 31.2 us -> 0 us
    psum x7 -> x0, blocking collectives: 325 us -> none  [the longest x3 215 us: on_device(): col_total = lax.psum(col_part, 'batch')]
    ppermute x0 -> x35, waiting for transfers between devices: none -> 53.8 us  [shifted(): lax.ppermute(value, axis, [(i, (i + shift) % size) for i in range(size)])]
    reduce_sum x9 -> x1, other arithmetic: 46.9 us -> 0.15 us  [on_device(): along = jnp.sum(unit_here * feat_sum, axis=1, keepdims=True)]
    psum x1 -> x0, waiting for transfers between devices: 45.9 us -> none  [on_device(): feat_sum = lax.psum(feat_part, 'proto')]
    ppermute x0 -> x35, starting transfers between devices: none -> 42.1 us  [shifted(): lax.ppermute(value, axis, [(i, (i + shift) % size) for i in range(size)])]
    pallas_call x0 -> x8, Pallas kernels: none -> 33.2 us  [the longest x1 13.9 us: grad_call(): pl.pallas_call(functools.partial(grad_kernel, total_protos=total_protos,...]
    dot_general x4 -> x0, matrix products: 31.2 us -> none  [the longest x1 11.5 us: on_device(): jnp.dot(teach_z, teach_w, preferred_element_type=jnp.float32) / TEACHER_TEMP]
    reduce_scatter x1, waiting for transfers between devices: 29.5 us -> 58.9 us  [on_device(): lax.psum_scatter(grad_part, BATCH, scatter_dimension=0, tiled=True)]
  transfers between devices with their start and end apart: 2 -> 36, of which waited for: 2 -> 21; matrix products, arithmetic and copies ran while one was open for 2% -> 2% of each run, Pallas kernels for 0% -> 2%
where the time goes in v1:
time: 216 us
  waiting for transfers between devices  113 us (52%)
  starting transfers between devices  42.1 us (19%)
  Pallas kernels  33.2 us (15%)
  between operations  14.4 us (7%)
  local copies, waits for them, and re-layouts  7.73 us (4%)
  other arithmetic  5.99 us (3%)
    reduce_scatter x1, waiting for transfers between devices, on_device(): lax.psum_scatter(grad_part, BATCH, scatter_dimension=0, tiled=True)  58.9 us
    ppermute x35, waiting for transfers between devices, shifted(): lax.ppermute(value, axis, [(i, (i + shift) % size) for i in range(size)])  53.8 us
    ppermute x35, starting transfers between devices, shifted(): lax.ppermute(value, axis, [(i, (i + shift) % size) for i in range(size)])  42.1 us
    pallas_call x1, Pallas kernels, grad_call(): pl.pallas_call(functools.partial(grad_kernel, total_protos=total_protos,...  13.9 us
    unnamed x6, local copies, waits for them, and re-layouts  7.63 us
    pallas_call x3, Pallas kernels, row_call(): pl.pallas_call(functools.partial(row_kernel, total_protos=total_protos),...  6.85 us
    pallas_call x1, Pallas kernels, student_call(): pl.pallas_call(functools.partial(student_kernel, size=size), grid=(count...  5.21 us
    pallas_call x1, Pallas kernels, energy_call(): pl.pallas_call(functools.partial(energy_kernel, size=size), grid=(count /...  4.79 us
  transfers between devices with their start and end apart: 36, of which 21 were waited for; matrix products, arithmetic and copies ran while one was open for 2% of the time, Pallas kernels for 2%

profile of v1, /device:TPU:0, one launch (start us, length us, event | category | flops | bytes accessed | tf_op | source)
XLA Modules:
  0.0 216.1 jit_solution(14968177455075910119)
XLA Ops:
  7.2 1.1 fusion
  9.4 2.2 %copy-done.1 = bf16[256,8192]{1,0:T(8,128)(2,1)S(1)} copy-done((bf16[256,8192]{1,0:T(8,128)(2,1)S(1)}, bf16[256,8192]{1,0:T(8,128)(2,1)}, u32[]{:S(2)}) %copy-start.1) | copy-done | bytes 4194328
  11.6 4.8 %energy.1 = (bf16[512,8192]{1,0:T(8,128)(2,1)S(1)}, f32[1,8192]{1,0:T(1,128)S(1)}) custom-call(bf16[512,256]{1,0:T(8,128)(2,1)S(1)} %fusion.1.feats, bf16[256,8192]{1,0:T(8,128)(2,1)S(1)} %copy-done.1), custom_call_target="tpu_custom_call" | custom-call | tf_op jit(solution)/shard_map/energy/pallas_call | solution.py:69
  16.4 1.6 collective-permute-start
  18.1 1.7 collective-permute-start.1
  19.7 1.9 collective-permute-start.2
  22.7 2.4 %collective-permute-done.2 = f32[1,8192]{1,0:T(1,128)S(1)} collective-permute-done((f32[1,8192]{1,0:T(1,128)S(1)}, f32[1,8192]{1,0:T(1,128)S(1)}, u32[]{:S(2)}, u32[]{:S(2)}) %collective-permute-start.2) | collective-permute-done | bytes 32800 | tf_op jit(solution)/shard_map/ppermute | solution.py:219
  25.2 2.1 collective-permute-start.3
  27.3 2.2 %collective-permute-start.4 = (f32[1,8192]{1,0:T(1,128)S(1)}, f32[1,8192]{1,0:T(1,128)S(1)}, u32[]{:S(2)}, u32[]{:S(2)}) collective-permute-start(f32[1,8192]{1,0:T(1,128)S(1)} %add_add_fusion.6), channel_id=1, source_target_pairs={{0,24},{8,0},{16,8},{24,16},{1,25},{9,1},{17,9},{25,17},{2,26},{10... | collective-permute-start | bytes 98312 | tf_op jit(solution)/shard_map/ppermute | solution.py:219
  29.5 1.8 collective-permute-start.5
  32.4 2.2 %copy-done.2 = bf16[256,8192]{1,0:T(8,128)(2,1)S(1)} copy-done((bf16[256,8192]{1,0:T(8,128)(2,1)S(1)}, bf16[256,8192]{1,0:T(8,128)(2,1)}, u32[]{:S(2)}) %copy-start.2) | copy-done | bytes 4194328
  34.5 5.2 %student.1 = (bf16[512,8192]{1,0:T(8,128)(2,1)S(1)}, bf16[256,8192]{1,0:T(8,128)(2,1)S(1)}, f32[1,8192]{1,0:T(1,128)S(1)}, f32[1,512]{1,0:T(1,128)S(1)}) custom-call(bf16[512,256]{1,0:T(8,128)(2,1)S(1)} %fusion.3.feats, bf16[256,8192]{1,0:T(8,128)(2,1)S(1)} %copy-done.2), custom_call_target="tpu_custom_call" | custom-call | tf_op jit(solution)/shard_map/student/pallas_call | solution.py:109
  39.9 2.3 %row_pass.3 = f32[1,512]{1,0:T(1,128)S(1)} custom-call(bf16[512,8192]{1,0:T(8,128)(2,1)S(1)} %get-tuple-element.10.energy, f32[1,8192]{1,0:T(1,128)S(1)} %add_add_fusion.5.col_total), custom_call_target="tpu_custom_call" | custom-call | tf_op jit(solution)/shard_map/row_pass/pallas_call | solution.py:138
  42.3 1.2 collective-permute-done.6
  43.4 1.7 collective-permute-start.7
  45.1 1.6 collective-permute-start.8
  46.7 2.0 collective-permute-start.9
  48.7 3.1 %collective-permute-done.9 = f32[2,512]{1,0:T(2,128)S(1)} collective-permute-done((f32[2,512]{1,0:T(2,128)S(1)}, f32[2,512]{1,0:T(2,128)S(1)}, u32[]{:S(2)}, u32[]{:S(2)}) %collective-permute-start.9) | collective-permute-done | bytes 4128 | tf_op jit(solution)/shard_map/ppermute | solution.py:219
  51.9 1.2 col_pass.2
  53.5 2.9 %collective-permute-start.11 = (f32[1,8192]{1,0:T(1,128)S(1)}, f32[1,8192]{1,0:T(1,128)S(1)}, u32[]{:S(2)}, u32[]{:S(2)}) collective-permute-start(f32[1,8192]{1,0:T(1,128)S(1)} %col_pass.2), channel_id=1, source_target_pairs={{0,96},{32,0},{64,32},{96,64},{1,97},{33,1},{65,33},{97,65},{2,98}... | collective-permute-start | bytes 98312 | tf_op jit(solution)/shard_map/ppermute | solution.py:219
  57.0 1.3 collective-permute-done.10
  58.3 3.5 %collective-permute-done.12 = f32[1,8192]{1,0:T(1,128)S(1)} collective-permute-done((f32[1,8192]{1,0:T(1,128)S(1)}, f32[1,8192]{1,0:T(1,128)S(1)}, u32[]{:S(2)}, u32[]{:S(2)}) %collective-permute-start.12) | collective-permute-done | bytes 32800 | tf_op jit(solution)/shard_map/ppermute | solution.py:219
  63.0 2.2 %collective-permute-start.14 = (f32[1,8192]{1,0:T(1,128)S(1)}, f32[1,8192]{1,0:T(1,128)S(1)}, u32[]{:S(2)}, u32[]{:S(2)}) collective-permute-start(f32[1,8192]{1,0:T(1,128)S(1)} %add_add_fusion.4), channel_id=1, source_target_pairs={{0,24},{8,0},{16,8},{24,16},{1,25},{9,1},{17,9},{25,17},{2,26},{10... | collective-permute-start | bytes 98312 | tf_op jit(solution)/shard_map/ppermute | solution.py:219
  65.7 1.3 collective-permute-done.13
  67.1 3.5 %collective-permute-done.15 = f32[1,8192]{1,0:T(1,128)S(1)} collective-permute-done((f32[1,8192]{1,0:T(1,128)S(1)}, f32[1,8192]{1,0:T(1,128)S(1)}, u32[]{:S(2)}, u32[]{:S(2)}) %collective-permute-start.15) | collective-permute-done | bytes 32800 | tf_op jit(solution)/shard_map/ppermute | solution.py:219
  70.7 2.3 %row_pass.4 = f32[1,512]{1,0:T(1,128)S(1)} custom-call(bf16[512,8192]{1,0:T(8,128)(2,1)S(1)} %get-tuple-element.10.energy, f32[1,8192]{1,0:T(1,128)S(1)} %add_add_fusion.3.col_total), custom_call_target="tpu_custom_call" | custom-call | tf_op jit(solution)/shard_map/row_pass/pallas_call | solution.py:138
  73.2 1.1 collective-permute-done.16
  74.8 2.8 %collective-permute-start.18 = (f32[1,512]{1,0:T(1,128)S(1)}, f32[1,512]{1,0:T(1,128)S(1)}, u32[]{:S(2)}, u32[]{:S(2)}) collective-permute-start(f32[1,512]{1,0:T(1,128)S(1)} %add.151), channel_id=1, source_target_pairs={{0,6},{2,0},{4,2},{6,4},{1,7},{3,1},{5,3},{7,5},{8,14},{10,8},{12,... | collective-permute-start | bytes 6152 | tf_op jit(solution)/shard_map/ppermute | solution.py:219
  79.2 3.5 %collective-permute-done.19 = f32[1,512]{1,0:T(1,128)S(1)} collective-permute-done((f32[1,512]{1,0:T(1,128)S(1)}, f32[1,512]{1,0:T(1,128)S(1)}, u32[]{:S(2)}, u32[]{:S(2)}) %collective-permute-start.19) | collective-permute-done | bytes 2080 | tf_op jit(solution)/shard_map/ppermute | solution.py:219
  82.7 1.2 col_pass.3
  84.0 3.2 %collective-permute-start.21 = (f32[1,8192]{1,0:T(1,128)S(1)}, f32[1,8192]{1,0:T(1,128)S(1)}, u32[]{:S(2)}, u32[]{:S(2)}) collective-permute-start(f32[1,8192]{1,0:T(1,128)S(1)} %col_pass.3), channel_id=1, source_target_pairs={{0,96},{32,0},{64,32},{96,64},{1,97},{33,1},{65,33},{97,65},{2,98}... | collective-permute-start | bytes 98312 | tf_op jit(solution)/shard_map/ppermute | solution.py:219
  87.2 1.9 collective-permute-done.20
  89.1 3.5 %collective-permute-done.22 = f32[1,8192]{1,0:T(1,128)S(1)} collective-permute-done((f32[1,8192]{1,0:T(1,128)S(1)}, f32[1,8192]{1,0:T(1,128)S(1)}, u32[]{:S(2)}, u32[]{:S(2)}) %collective-permute-start.22) | collective-permute-done | bytes 32800 | tf_op jit(solution)/shard_map/ppermute | solution.py:219
  92.8 3.2 %collective-permute-start.24 = (f32[1,8192]{1,0:T(1,128)S(1)}, f32[1,8192]{1,0:T(1,128)S(1)}, u32[]{:S(2)}, u32[]{:S(2)}) collective-permute-start(f32[1,8192]{1,0:T(1,128)S(1)} %add_add_fusion.2), channel_id=1, source_target_pairs={{0,24},{8,0},{16,8},{24,16},{1,25},{9,1},{17,9},{25,17},{2,26},{10... | collective-permute-start | bytes 98312 | tf_op jit(solution)/shard_map/ppermute | solution.py:219
  96.0 1.9 collective-permute-done.23
  97.9 3.5 %collective-permute-done.25 = f32[1,8192]{1,0:T(1,128)S(1)} collective-permute-done((f32[1,8192]{1,0:T(1,128)S(1)}, f32[1,8192]{1,0:T(1,128)S(1)}, u32[]{:S(2)}, u32[]{:S(2)}) %collective-permute-start.25) | collective-permute-done | bytes 32800 | tf_op jit(solution)/shard_map/ppermute | solution.py:219
  101.5 2.3 %row_pass.5 = f32[1,512]{1,0:T(1,128)S(1)} custom-call(bf16[512,8192]{1,0:T(8,128)(2,1)S(1)} %get-tuple-element.10.energy, f32[1,8192]{1,0:T(1,128)S(1)} %add_add_fusion.1.col_total), custom_call_target="tpu_custom_call" | custom-call | tf_op jit(solution)/shard_map/row_pass/pallas_call | solution.py:138
  103.9 1.1 collective-permute-done.26
  105.0 3.2 %collective-permute-start.28 = (f32[1,512]{1,0:T(1,128)S(1)}, f32[1,512]{1,0:T(1,128)S(1)}, u32[]{:S(2)}, u32[]{:S(2)}) collective-permute-start(f32[1,512]{1,0:T(1,128)S(1)} %add.161), channel_id=1, source_target_pairs={{0,6},{2,0},{4,2},{6,4},{1,7},{3,1},{5,3},{7,5},{8,14},{10,8},{12,... | collective-permute-start | bytes 6152 | tf_op jit(solution)/shard_map/ppermute | solution.py:219
  108.3 1.6 collective-permute-done.27
  109.8 3.5 %collective-permute-done.29 = f32[1,512]{1,0:T(1,128)S(1)} collective-permute-done((f32[1,512]{1,0:T(1,128)S(1)}, f32[1,512]{1,0:T(1,128)S(1)}, u32[]{:S(2)}, u32[]{:S(2)}) %collective-permute-start.29) | collective-permute-done | bytes 2080 | tf_op jit(solution)/shard_map/ppermute | solution.py:219
  113.4 13.9 %grad.1 = (f32[512,256]{1,0:T(8,128)S(1)}, f32[256,8192]{1,0:T(8,128)S(1)}) custom-call(bf16[512,8192]{1,0:T(8,128)(2,1)S(1)} %get-tuple-element.10.energy, bf16[512,8192]{1,0:T(8,128)(2,1)S(1)} %get-tuple-element.11.expo, bf16[512,256]{1,0:T(8,128)(2,1)S(1)} %fusion.3.feats, bf16[256,8192]{1,0:T(8,128)(2,1)S(1)} %get-tuple-element.12.unit, ...), custom_call_target="tpu_custom_call" | custom-call | tf_op jit(solution)/shard_map/grad/pallas_call | solution.py:205
  127.3 3.3 %copy-done = f32[256,8192]{1,0:T(8,128)} copy-done((f32[256,8192]{1,0:T(8,128)}, f32[256,8192]{1,0:T(8,128)S(1)}, u32[]{:S(2)}) %copy-start) | copy-done | bytes 8388632
  130.7 1.5 collective-permute-done.30
  132.3 3.2 %collective-permute-start.32 = (f32[256,256]{1,0:T(8,128)S(1)}, f32[256,256]{1,0:T(8,128)S(1)}, u32[]{:S(2)}, u32[]{:S(2)}) collective-permute-start(f32[256,256]{1,0:T(8,128)S(1)} %dynamic-slice_add_fusion), channel_id=1, source_target_pairs={{0,6},{2,0},{4,2},{6,4},{1,7},{3,1},{5,3},{7,5},{8,14},{10,8},{12,... | collective-permute-start | bytes 786440 | tf_op jit(solution)/shard_map/ppermute | solution.py:219
  135.6 11.9 %collective-permute-done.31 = f32[256,256]{1,0:T(8,128)S(1)} collective-permute-done((f32[256,256]{1,0:T(8,128)S(1)}, f32[256,256]{1,0:T(8,128)S(1)}, u32[]{:S(2)}, u32[]{:S(2)}) %collective-permute-start.31) | collective-permute-done | bytes 262176 | tf_op jit(solution)/shard_map/ppermute | solution.py:219
  147.9 1.5 collective-permute-done.34
  150.3 58.9 %reduce-scatter.2.cloned.1.call-done = f32[16,8192]{1,0:T(8,128)} async-done(((f32[256,8192]{1,0:T(8,128)}), f32[16,8192]{1,0:T(8,128)}) %reduce-scatter.2.cloned.1.call-update) | async-done | bytes 524304 | tf_op jit(solution)/shard_map/reduce_scatter | solution.py:253
  (66 shorter events, 10.5 us)
Async XLA Ops:
  7.2 202.1 %reduce-scatter.2.cloned.1.call-start = ((), (), s32[]{:S(2)}) async-start(), calls=%async_computation.1 | async-start | bytes 8912896 | tf_op jit(solution)/shard_map/reduce_scatter | solution.py:253
  9.4 2.2 %copy-start.1 = (bf16[256,8192]{1,0:T(8,128)(2,1)S(1)}, bf16[256,8192]{1,0:T(8,128)(2,1)}, u32[]{:S(2)}) copy-start(bf16[256,8192]{1,0:T(8,128)(2,1)} %protos.2) | copy-start | bytes 12582916
  16.4 6.3 %collective-permute-start = (f32[1,8192]{1,0:T(1,128)S(1)}, f32[1,8192]{1,0:T(1,128)S(1)}, u32[]{:S(2)}, u32[]{:S(2)}) collective-permute-start(f32[1,8192]{1,0:T(1,128)S(1)} %get-tuple-element.14), channel_id=1, source_target_pairs={{0,32},{32,64},{64,96},{96,0},{1,33},{33,65},{65,97},{97,1},{2,34}... | collective-permute-start | bytes 98312 | tf_op jit(solution)/shard_map/ppermute | solution.py:219
  18.1 4.7 %collective-permute-start.1 = (f32[1,8192]{1,0:T(1,128)S(1)}, f32[1,8192]{1,0:T(1,128)S(1)}, u32[]{:S(2)}, u32[]{:S(2)}) collective-permute-start(f32[1,8192]{1,0:T(1,128)S(1)} %get-tuple-element.14), channel_id=1, source_target_pairs={{0,96},{32,0},{64,32},{96,64},{1,97},{33,1},{65,33},{97,65},{2,98}... | collective-permute-start | bytes 98312 | tf_op jit(solution)/shard_map/ppermute | solution.py:219
  19.7 5.4 %collective-permute-start.2 = (f32[1,8192]{1,0:T(1,128)S(1)}, f32[1,8192]{1,0:T(1,128)S(1)}, u32[]{:S(2)}, u32[]{:S(2)}) collective-permute-start(f32[1,8192]{1,0:T(1,128)S(1)} %get-tuple-element.14), channel_id=1, source_target_pairs={{0,64},{32,96},{64,0},{96,32},{1,65},{33,97},{65,1},{97,33},{2,66}... | collective-permute-start | bytes 98312 | tf_op jit(solution)/shard_map/ppermute | solution.py:219
  25.2 14.6 %collective-permute-start.3 = (f32[1,8192]{1,0:T(1,128)S(1)}, f32[1,8192]{1,0:T(1,128)S(1)}, u32[]{:S(2)}, u32[]{:S(2)}) collective-permute-start(f32[1,8192]{1,0:T(1,128)S(1)} %add_add_fusion.6), channel_id=1, source_target_pairs={{0,8},{8,16},{16,24},{24,0},{1,9},{9,17},{17,25},{25,1},{2,10},{10... | collective-permute-start | bytes 98312 | tf_op jit(solution)/shard_map/ppermute | solution.py:219
  27.3 12.5 %collective-permute-start.4 = (f32[1,8192]{1,0:T(1,128)S(1)}, f32[1,8192]{1,0:T(1,128)S(1)}, u32[]{:S(2)}, u32[]{:S(2)}) collective-permute-start(f32[1,8192]{1,0:T(1,128)S(1)} %add_add_fusion.6), channel_id=1, source_target_pairs={{0,24},{8,0},{16,8},{24,16},{1,25},{9,1},{17,9},{25,17},{2,26},{10... | collective-permute-start | bytes 98312 | tf_op jit(solution)/shard_map/ppermute | solution.py:219
  29.5 10.3 %collective-permute-start.5 = (f32[1,8192]{1,0:T(1,128)S(1)}, f32[1,8192]{1,0:T(1,128)S(1)}, u32[]{:S(2)}, u32[]{:S(2)}) collective-permute-start(f32[1,8192]{1,0:T(1,128)S(1)} %add_add_fusion.6), channel_id=1, source_target_pairs={{0,16},{8,24},{16,0},{24,8},{1,17},{9,25},{17,1},{25,9},{2,18},{10... | collective-permute-start | bytes 98312 | tf_op jit(solution)/shard_map/ppermute | solution.py:219
  32.3 2.2 %copy-start.2 = (bf16[256,8192]{1,0:T(8,128)(2,1)S(1)}, bf16[256,8192]{1,0:T(8,128)(2,1)}, u32[]{:S(2)}) copy-start(bf16[256,8192]{1,0:T(8,128)(2,1)} %protos.3) | copy-start | bytes 12582916
  42.2 1.2 collective-permute-start.6
  43.4 5.3 %collective-permute-start.7 = (f32[2,512]{1,0:T(2,128)S(1)}, f32[2,512]{1,0:T(2,128)S(1)}, u32[]{:S(2)}, u32[]{:S(2)}) collective-permute-start(f32[2,512]{1,0:T(2,128)S(1)} %fusion.7), channel_id=1, source_target_pairs={{0,2},{2,4},{4,6},{6,0},{1,3},{3,5},{5,7},{7,1},{8,10},{10,12},{12... | collective-permute-start | bytes 12296 | tf_op jit(solution)/shard_map/ppermute | solution.py:219
  45.1 3.6 %collective-permute-start.8 = (f32[2,512]{1,0:T(2,128)S(1)}, f32[2,512]{1,0:T(2,128)S(1)}, u32[]{:S(2)}, u32[]{:S(2)}) collective-permute-start(f32[2,512]{1,0:T(2,128)S(1)} %fusion.7), channel_id=1, source_target_pairs={{0,6},{2,0},{4,2},{6,4},{1,7},{3,1},{5,3},{7,5},{8,14},{10,8},{12,... | collective-permute-start | bytes 12296 | tf_op jit(solution)/shard_map/ppermute | solution.py:219
  46.7 5.1 %collective-permute-start.9 = (f32[2,512]{1,0:T(2,128)S(1)}, f32[2,512]{1,0:T(2,128)S(1)}, u32[]{:S(2)}, u32[]{:S(2)}) collective-permute-start(f32[2,512]{1,0:T(2,128)S(1)} %fusion.7), channel_id=1, source_target_pairs={{0,4},{2,6},{4,0},{6,2},{1,5},{3,7},{5,1},{7,3},{8,12},{10,14},{12... | collective-permute-start | bytes 12296 | tf_op jit(solution)/shard_map/ppermute | solution.py:219
  53.1 5.2 %collective-permute-start.10 = (f32[1,8192]{1,0:T(1,128)S(1)}, f32[1,8192]{1,0:T(1,128)S(1)}, u32[]{:S(2)}, u32[]{:S(2)}) collective-permute-start(f32[1,8192]{1,0:T(1,128)S(1)} %col_pass.2), channel_id=1, source_target_pairs={{0,32},{32,64},{64,96},{96,0},{1,33},{33,65},{65,97},{97,1},{2,34}... | collective-permute-start | bytes 98312 | tf_op jit(solution)/shard_map/ppermute | solution.py:219
  53.5 4.8 %collective-permute-start.11 = (f32[1,8192]{1,0:T(1,128)S(1)}, f32[1,8192]{1,0:T(1,128)S(1)}, u32[]{:S(2)}, u32[]{:S(2)}) collective-permute-start(f32[1,8192]{1,0:T(1,128)S(1)} %col_pass.2), channel_id=1, source_target_pairs={{0,96},{32,0},{64,32},{96,64},{1,97},{33,1},{65,33},{97,65},{2,98}... | collective-permute-start | bytes 98312 | tf_op jit(solution)/shard_map/ppermute | solution.py:219
  56.4 5.4 %collective-permute-start.12 = (f32[1,8192]{1,0:T(1,128)S(1)}, f32[1,8192]{1,0:T(1,128)S(1)}, u32[]{:S(2)}, u32[]{:S(2)}) collective-permute-start(f32[1,8192]{1,0:T(1,128)S(1)} %col_pass.2), channel_id=1, source_target_pairs={{0,64},{32,96},{64,0},{96,32},{1,65},{33,97},{65,1},{97,33},{2,66}... | collective-permute-start | bytes 98312 | tf_op jit(solution)/shard_map/ppermute | solution.py:219
  61.9 5.2 %collective-permute-start.13 = (f32[1,8192]{1,0:T(1,128)S(1)}, f32[1,8192]{1,0:T(1,128)S(1)}, u32[]{:S(2)}, u32[]{:S(2)}) collective-permute-start(f32[1,8192]{1,0:T(1,128)S(1)} %add_add_fusion.4), channel_id=1, source_target_pairs={{0,8},{8,16},{16,24},{24,0},{1,9},{9,17},{17,25},{25,1},{2,10},{10... | collective-permute-start | bytes 98312 | tf_op jit(solution)/shard_map/ppermute | solution.py:219
  63.0 4.1 %collective-permute-start.14 = (f32[1,8192]{1,0:T(1,128)S(1)}, f32[1,8192]{1,0:T(1,128)S(1)}, u32[]{:S(2)}, u32[]{:S(2)}) collective-permute-start(f32[1,8192]{1,0:T(1,128)S(1)} %add_add_fusion.4), channel_id=1, source_target_pairs={{0,24},{8,0},{16,8},{24,16},{1,25},{9,1},{17,9},{25,17},{2,26},{10... | collective-permute-start | bytes 98312 | tf_op jit(solution)/shard_map/ppermute | solution.py:219
  65.2 5.4 %collective-permute-start.15 = (f32[1,8192]{1,0:T(1,128)S(1)}, f32[1,8192]{1,0:T(1,128)S(1)}, u32[]{:S(2)}, u32[]{:S(2)}) collective-permute-start(f32[1,8192]{1,0:T(1,128)S(1)} %add_add_fusion.4), channel_id=1, source_target_pairs={{0,16},{8,24},{16,0},{24,8},{1,17},{9,25},{17,1},{25,9},{2,18},{10... | collective-permute-start | bytes 98312 | tf_op jit(solution)/shard_map/ppermute | solution.py:219
  73.0 1.4 collective-permute-start.16
  74.4 4.8 %collective-permute-start.17 = (f32[1,512]{1,0:T(1,128)S(1)}, f32[1,512]{1,0:T(1,128)S(1)}, u32[]{:S(2)}, u32[]{:S(2)}) collective-permute-start(f32[1,512]{1,0:T(1,128)S(1)} %add.151), channel_id=1, source_target_pairs={{0,2},{2,4},{4,6},{6,0},{1,3},{3,5},{5,7},{7,1},{8,10},{10,12},{12... | collective-permute-start | bytes 6152 | tf_op jit(solution)/shard_map/ppermute | solution.py:219
  74.8 4.4 %collective-permute-start.18 = (f32[1,512]{1,0:T(1,128)S(1)}, f32[1,512]{1,0:T(1,128)S(1)}, u32[]{:S(2)}, u32[]{:S(2)}) collective-permute-start(f32[1,512]{1,0:T(1,128)S(1)} %add.151), channel_id=1, source_target_pairs={{0,6},{2,0},{4,2},{6,4},{1,7},{3,1},{5,3},{7,5},{8,14},{10,8},{12,... | collective-permute-start | bytes 6152 | tf_op jit(solution)/shard_map/ppermute | solution.py:219
  77.6 5.1 %collective-permute-start.19 = (f32[1,512]{1,0:T(1,128)S(1)}, f32[1,512]{1,0:T(1,128)S(1)}, u32[]{:S(2)}, u32[]{:S(2)}) collective-permute-start(f32[1,512]{1,0:T(1,128)S(1)} %add.151), channel_id=1, source_target_pairs={{0,4},{2,6},{4,0},{6,2},{1,5},{3,7},{5,1},{7,3},{8,12},{10,14},{12... | collective-permute-start | bytes 6152 | tf_op jit(solution)/shard_map/ppermute | solution.py:219
  83.9 5.2 %collective-permute-start.20 = (f32[1,8192]{1,0:T(1,128)S(1)}, f32[1,8192]{1,0:T(1,128)S(1)}, u32[]{:S(2)}, u32[]{:S(2)}) collective-permute-start(f32[1,8192]{1,0:T(1,128)S(1)} %col_pass.3), channel_id=1, source_target_pairs={{0,32},{32,64},{64,96},{96,0},{1,33},{33,65},{65,97},{97,1},{2,34}... | collective-permute-start | bytes 98312 | tf_op jit(solution)/shard_map/ppermute | solution.py:219
  84.0 5.1 %collective-permute-start.21 = (f32[1,8192]{1,0:T(1,128)S(1)}, f32[1,8192]{1,0:T(1,128)S(1)}, u32[]{:S(2)}, u32[]{:S(2)}) collective-permute-start(f32[1,8192]{1,0:T(1,128)S(1)} %col_pass.3), channel_id=1, source_target_pairs={{0,96},{32,0},{64,32},{96,64},{1,97},{33,1},{65,33},{97,65},{2,98}... | collective-permute-start | bytes 98312 | tf_op jit(solution)/shard_map/ppermute | solution.py:219
  87.2 5.4 %collective-permute-start.22 = (f32[1,8192]{1,0:T(1,128)S(1)}, f32[1,8192]{1,0:T(1,128)S(1)}, u32[]{:S(2)}, u32[]{:S(2)}) collective-permute-start(f32[1,8192]{1,0:T(1,128)S(1)} %col_pass.3), channel_id=1, source_target_pairs={{0,64},{32,96},{64,0},{96,32},{1,65},{33,97},{65,1},{97,33},{2,66}... | collective-permute-start | bytes 98312 | tf_op jit(solution)/shard_map/ppermute | solution.py:219
  92.7 5.2 %collective-permute-start.23 = (f32[1,8192]{1,0:T(1,128)S(1)}, f32[1,8192]{1,0:T(1,128)S(1)}, u32[]{:S(2)}, u32[]{:S(2)}) collective-permute-start(f32[1,8192]{1,0:T(1,128)S(1)} %add_add_fusion.2), channel_id=1, source_target_pairs={{0,8},{8,16},{16,24},{24,0},{1,9},{9,17},{17,25},{25,1},{2,10},{10... | collective-permute-start | bytes 98312 | tf_op jit(solution)/shard_map/ppermute | solution.py:219
  92.8 5.1 %collective-permute-start.24 = (f32[1,8192]{1,0:T(1,128)S(1)}, f32[1,8192]{1,0:T(1,128)S(1)}, u32[]{:S(2)}, u32[]{:S(2)}) collective-permute-start(f32[1,8192]{1,0:T(1,128)S(1)} %add_add_fusion.2), channel_id=1, source_target_pairs={{0,24},{8,0},{16,8},{24,16},{1,25},{9,1},{17,9},{25,17},{2,26},{10... | collective-permute-start | bytes 98312 | tf_op jit(solution)/shard_map/ppermute | solution.py:219
  96.0 5.4 %collective-permute-start.25 = (f32[1,8192]{1,0:T(1,128)S(1)}, f32[1,8192]{1,0:T(1,128)S(1)}, u32[]{:S(2)}, u32[]{:S(2)}) collective-permute-start(f32[1,8192]{1,0:T(1,128)S(1)} %add_add_fusion.2), channel_id=1, source_target_pairs={{0,16},{8,24},{16,0},{24,8},{1,17},{9,25},{17,1},{25,9},{2,18},{10... | collective-permute-start | bytes 98312 | tf_op jit(solution)/shard_map/ppermute | solution.py:219
  103.8 1.2 collective-permute-start.26
  105.0 4.8 %collective-permute-start.27 = (f32[1,512]{1,0:T(1,128)S(1)}, f32[1,512]{1,0:T(1,128)S(1)}, u32[]{:S(2)}, u32[]{:S(2)}) collective-permute-start(f32[1,512]{1,0:T(1,128)S(1)} %add.161), channel_id=1, source_target_pairs={{0,2},{2,4},{4,6},{6,0},{1,3},{3,5},{5,7},{7,1},{8,10},{10,12},{12... | collective-permute-start | bytes 6152 | tf_op jit(solution)/shard_map/ppermute | solution.py:219
  105.0 4.8 %collective-permute-start.28 = (f32[1,512]{1,0:T(1,128)S(1)}, f32[1,512]{1,0:T(1,128)S(1)}, u32[]{:S(2)}, u32[]{:S(2)}) collective-permute-start(f32[1,512]{1,0:T(1,128)S(1)} %add.161), channel_id=1, source_target_pairs={{0,6},{2,0},{4,2},{6,4},{1,7},{3,1},{5,3},{7,5},{8,14},{10,8},{12,... | collective-permute-start | bytes 6152 | tf_op jit(solution)/shard_map/ppermute | solution.py:219
  108.3 5.1 %collective-permute-start.29 = (f32[1,512]{1,0:T(1,128)S(1)}, f32[1,512]{1,0:T(1,128)S(1)}, u32[]{:S(2)}, u32[]{:S(2)}) collective-permute-start(f32[1,512]{1,0:T(1,128)S(1)} %add.161), channel_id=1, source_target_pairs={{0,4},{2,6},{4,0},{6,2},{1,5},{3,7},{5,1},{7,3},{8,12},{10,14},{12... | collective-permute-start | bytes 6152 | tf_op jit(solution)/shard_map/ppermute | solution.py:219
  127.3 3.3 %copy-start = (f32[256,8192]{1,0:T(8,128)}, f32[256,8192]{1,0:T(8,128)S(1)}, u32[]{:S(2)}) copy-start(f32[256,8192]{1,0:T(8,128)S(1)} %get-tuple-element.17) | copy-start | bytes 25165828
  130.6 1.6 collective-permute-start.30
  132.3 15.2 %collective-permute-start.31 = (f32[256,256]{1,0:T(8,128)S(1)}, f32[256,256]{1,0:T(8,128)S(1)}, u32[]{:S(2)}, u32[]{:S(2)}) collective-permute-start(f32[256,256]{1,0:T(8,128)S(1)} %dynamic-slice_add_fusion), channel_id=1, source_target_pairs={{0,2},{2,4},{4,6},{6,0},{1,3},{3,5},{5,7},{7,1},{8,10},{10,12},{12... | collective-permute-start | bytes 786440 | tf_op jit(solution)/shard_map/ppermute | solution.py:219
  132.3 15.2 %collective-permute-start.32 = (f32[256,256]{1,0:T(8,128)S(1)}, f32[256,256]{1,0:T(8,128)S(1)}, u32[]{:S(2)}, u32[]{:S(2)}) collective-permute-start(f32[256,256]{1,0:T(8,128)S(1)} %dynamic-slice_add_fusion), channel_id=1, source_target_pairs={{0,6},{2,0},{4,2},{6,4},{1,7},{3,1},{5,3},{7,5},{8,14},{10,8},{12,... | collective-permute-start | bytes 786440 | tf_op jit(solution)/shard_map/ppermute | solution.py:219
  135.6 11.9 %collective-permute-start.33 = (f32[256,256]{1,0:T(8,128)S(1)}, f32[256,256]{1,0:T(8,128)S(1)}, u32[]{:S(2)}, u32[]{:S(2)}) collective-permute-start(f32[256,256]{1,0:T(8,128)S(1)} %dynamic-slice_add_fusion), channel_id=1, source_target_pairs={{0,4},{2,6},{4,0},{6,2},{1,5},{3,7},{5,1},{7,3},{8,12},{10,14},{12... | collective-permute-start | bytes 786440 | tf_op jit(solution)/shard_map/ppermute | solution.py:219
  147.8 1.6 collective-permute-start.34
Sparse Core Ops, SparseCore 0:
  130.7 78.4 reduce-scatter.1
